TPU v7x, 32 devices: a whole 2x2x4 slice. The times are simulated.
32 devices in a mesh: shard: 4 (over x, core), rep: 8 (over z, y).
Axes of the slice: x: 2, y: 2, z: 4, core: 2. Of those that a mesh axis runs over, the one named last changes fastest.
Arguments:
- tokens: bfloat16 [4096, 1024], P(('shard', 'rep')), may hold values from -6 to 6
- cotangent: bfloat16 [4096, 1024], P(('shard', 'rep')), may hold values from -6 to 6
- first_gain: bfloat16 [1024], P('shard'), may hold values from 0.099609375 to 1.8984375
- mixer_gate: bfloat16 [1024, 1536], P('shard'), may hold values from -0.1875 to 0.1875
- mixer_input: bfloat16 [1024, 1792], P('shard'), may hold values from -0.1875 to 0.1875
- step_weight: bfloat16 [1024, 24], P('shard'), may hold values from -0.1875 to 0.1875
- conv_weight: bfloat16 [4, 1792], P(None, 'shard'), may hold values from -3 to 3
- conv_bias: bfloat16 [1792], P('shard'), may hold values from -3 to 3
- step_bias: bfloat16 [24], P('shard'), may hold values from -6 to -2
- decay_log: bfloat16 [24], P('shard'), may hold values from 0 to 2.6875
- skip_weight: bfloat16 [24], P('shard'), may hold values from 0.5 to 2
- mixer_gain: bfloat16 [1536], P('shard'), may hold values from 0.099609375 to 1.8984375
- mixer_output: bfloat16 [1536, 1024], P('shard'), may hold values from -0.15625 to 0.15625
- query_matrix: bfloat16 [1024, 512], P('shard'), may hold values from -0.1875 to 0.1875
- key_matrix: bfloat16 [1024, 128], P('shard'), may hold values from -0.1875 to 0.1875
- value_matrix: bfloat16 [1024, 128], P('shard'), may hold values from -0.1875 to 0.1875
- attn_output: bfloat16 [512, 1024], P('shard'), may hold values from -1 to 1
- second_gain: bfloat16 [1024], P('shard'), may hold values from 0.099609375 to 1.8984375
- ffn_gate: bfloat16 [1024, 2048], P('shard'), may hold values from -0.1875 to 0.1875
- ffn_up: bfloat16 [1024, 2048], P('shard'), may hold values from -0.1875 to 0.1875
- ffn_down: bfloat16 [2048, 1024], P('shard'), may hold values from -0.125 to 0.125
Outputs:
- block_output: bfloat16 [4096, 1024], P(('shard', 'rep'))
- tokens_grad: bfloat16 [4096, 1024], P(('shard', 'rep'))
- grad_first_gain: float32 [1024], P(('shard', 'rep'))
- grad_mixer_gate: float32 [1024, 1536], P(('shard', 'rep'))
- grad_mixer_input: float32 [1024, 1792], P(('shard', 'rep'))
- grad_step_weight: float32 [1024, 24], P(('shard', 'rep'))
- grad_conv_weight: float32 [4, 1792], P(None, ('shard', 'rep'))
- grad_conv_bias: float32 [1792], P(('shard', 'rep'))
- grad_step_bias: float32 [24], P('shard')
- grad_decay_log: float32 [24], P('shard')
- grad_skip_weight: float32 [24], P('shard')
- grad_mixer_gain: float32 [1536], P(('shard', 'rep'))
- grad_mixer_output: float32 [1536, 1024], P(('shard', 'rep'))
- grad_query_weight: float32 [1024, 512], P(('shard', 'rep'))
- grad_key_weight: float32 [1024, 128], P(('shard', 'rep'))
- grad_value_weight: float32 [1024, 128], P(('shard', 'rep'))
- grad_attn_output: float32 [512, 1024], P(('shard', 'rep'))
- grad_second_gain: float32 [1024], P(('shard', 'rep'))
- grad_ffn_gate: float32 [1024, 2048], P(('shard', 'rep'))
- grad_ffn_up: float32 [1024, 2048], P(('shard', 'rep'))
- grad_ffn_down: float32 [2048, 1024], P(('shard', 'rep'))
All inputs are finite; a program needn't handle non-finite values.
Results may differ from a plain program's by a relative error of at most 0.017.
Values may be sent and summed in bfloat16 or wider, within the bound.
No kernel may reach another device: no remote copies, remote signals or barrier semaphores. Data moves between devices by JAX's collectives and lax.ppermute only.
A program may use at most 192 MiB of HBM per device.

v0:
```python
import jax
import jax.numpy as jnp
from jax import lax
from jax.sharding import PartitionSpec as P

QUERY_HEADS = 8
KEY_VALUE_HEADS = 2
HEAD_WIDTH = 64
HM = 24
P_SIZE = 64
N = 128
KC = 4
SEQUENCE_LENGTH = 128
DS = 1536


EPS = 1e-05
HIGH = lax.Precision.HIGHEST
REDUCED_DTYPE = jnp.bfloat16
WIDER = jnp.float32


def rms_scale(values, gain):
    return values * lax.rsqrt(jnp.mean(values * values, axis=-1, keepdims=True) + EPS) * gain


def swiglu(gate_value, up_value):
    return jax.nn.silu(gate_value) * up_value


def mixer_core(
    gate_in,
    mixed_in,
    step_in,
    kernel_taps,
    kernel_offset,
    step_offset,
    decay_rates,
    skip_scale,
    norm_gain,
):
    batch_count, token_length = (mixed_in.shape[0], mixed_in.shape[1])
    padded = jnp.pad(mixed_in, ((0, 0), (KC - 1, 0), (0, 0)))
    convolved = kernel_offset + padded[:, 0:token_length] * kernel_taps[0]
    for offset in range(1, KC):
        convolved = convolved + padded[:, offset : offset + token_length] * kernel_taps[offset]
    active = jax.nn.silu(convolved)
    inner_values = active[:, :, :DS].reshape(batch_count, token_length, HM, P_SIZE)
    in_state = active[:, :, DS : DS + N]
    out_state = active[:, :, DS + N :]
    step_size = jax.nn.softplus(step_in + step_offset)
    log_decay = -step_size * jnp.exp(decay_rates)
    running = jnp.cumsum(log_decay, axis=1)
    positions = jnp.arange(token_length)
    causal = (positions[:, None] >= positions[None, :])[None, :, :, None]
    spread = running[:, :, None, :] - running[:, None, :, :]
    decay_factor = jnp.where(causal, jnp.exp(jnp.where(causal, spread, 0.0)), 0.0)
    coupling = jnp.einsum("btn,bsn->bts", out_state, in_state, precision=HIGH)
    mixing = coupling[:, :, :, None] * decay_factor * step_size[:, None, :, :]
    result = (
        jnp.einsum("btsh,bshp->bthp", mixing, inner_values, precision=HIGH)
        + skip_scale[:, None] * inner_values
    )
    gated_values = result.reshape(batch_count, token_length, DS) * jax.nn.silu(gate_in)
    return rms_scale(gated_values, norm_gain)


def matmul(left, right):
    return jnp.dot(left, right, preferred_element_type=WIDER)


def weight_grad(left, grad):
    return lax.dot_general(left, grad, (((0,), (0,)), ((), ())), preferred_element_type=WIDER)


def input_gradient(grad, weight):
    return lax.dot_general(grad, weight, (((1,), (1,)), ((), ())), preferred_element_type=WIDER)


def attention_scores(query_head_rows, key_head_rows, token_length):
    positions = jnp.arange(token_length)
    causal = positions[:, None] >= positions[None, :]
    raw = jnp.einsum(
        "bqkjd,bskd->bkjqs", query_head_rows, key_head_rows, preferred_element_type=WIDER
    )
    return jnp.where(causal, raw * HEAD_WIDTH ** (-0.5), -1e30)


def local(
    tokens,
    cotangent,
    first_gain,
    mixer_gate,
    mixer_input,
    step_weight,
    conv_weight,
    conv_bias,
    step_bias,
    decay_log,
    skip_weight,
    mixer_gain,
    mixer_output,
    query_matrix,
    key_matrix,
    value_matrix,
    attn_output,
    second_gain,
    ffn_gate,
    ffn_up,
    ffn_down,
):
    gathered = (
        lax.all_gather(first_gain, "shard", axis=0, tiled=True),
        lax.all_gather(mixer_gate, "shard", axis=0, tiled=True),
        lax.all_gather(mixer_input, "shard", axis=0, tiled=True),
        lax.all_gather(step_weight, "shard", axis=0, tiled=True),
        lax.all_gather(conv_weight, "shard", axis=1, tiled=True),
        lax.all_gather(conv_bias, "shard", axis=0, tiled=True),
        lax.all_gather(step_bias, "shard", axis=0, tiled=True),
        lax.all_gather(decay_log, "shard", axis=0, tiled=True),
        lax.all_gather(skip_weight, "shard", axis=0, tiled=True),
        lax.all_gather(mixer_gain, "shard", axis=0, tiled=True),
        lax.all_gather(mixer_output, "shard", axis=0, tiled=True),
        lax.all_gather(query_matrix, "shard", axis=0, tiled=True),
        lax.all_gather(key_matrix, "shard", axis=0, tiled=True),
        lax.all_gather(value_matrix, "shard", axis=0, tiled=True),
        lax.all_gather(attn_output, "shard", axis=0, tiled=True),
        lax.all_gather(second_gain, "shard", axis=0, tiled=True),
        lax.all_gather(ffn_gate, "shard", axis=0, tiled=True),
        lax.all_gather(ffn_up, "shard", axis=0, tiled=True),
        lax.all_gather(ffn_down, "shard", axis=0, tiled=True),
    )
    token_rows = tokens.shape[0]
    batch_count = token_rows // SEQUENCE_LENGTH
    shard_groups = QUERY_HEADS // KEY_VALUE_HEADS
    inputs = tokens.astype(WIDER)
    norm_one, norm_one_back = jax.vjp(rms_scale, inputs, gathered[0].astype(WIDER))
    normalized_input = norm_one.astype(REDUCED_DTYPE)
    gate_in = matmul(normalized_input, gathered[1])
    mixed_in = matmul(normalized_input, gathered[2])
    step_in = matmul(normalized_input, gathered[3])

    def mixer_rows(
        gate_part,
        mixed_part,
        step_part,
        kernel_taps,
        kernel_offset,
        step_offset,
        decay_rates,
        skip_scale,
        norm_gain,
    ):
        value = mixer_core(
            gate_part.reshape(batch_count, SEQUENCE_LENGTH, -1),
            mixed_part.reshape(batch_count, SEQUENCE_LENGTH, -1),
            step_part.reshape(batch_count, SEQUENCE_LENGTH, -1),
            kernel_taps,
            kernel_offset,
            step_offset,
            decay_rates,
            skip_scale,
            norm_gain,
        )
        return value.reshape(token_rows, -1)

    mixer_value, mixer_back = jax.vjp(
        mixer_rows,
        gate_in,
        mixed_in,
        step_in,
        gathered[4].astype(WIDER),
        gathered[5].astype(WIDER),
        gathered[6].astype(WIDER),
        gathered[7].astype(WIDER),
        gathered[8].astype(WIDER),
        gathered[9].astype(WIDER),
    )
    mixer_norm = mixer_value.astype(REDUCED_DTYPE)
    mixer_term = matmul(mixer_norm, gathered[10])
    query_reduced = matmul(normalized_input, gathered[11]).astype(REDUCED_DTYPE)
    key_reduced = matmul(normalized_input, gathered[12]).astype(REDUCED_DTYPE)
    value_reduced = matmul(normalized_input, gathered[13]).astype(REDUCED_DTYPE)
    query_head_rows = query_reduced.reshape(
        batch_count, SEQUENCE_LENGTH, KEY_VALUE_HEADS, shard_groups, HEAD_WIDTH
    )
    key_head_rows = key_reduced.reshape(batch_count, SEQUENCE_LENGTH, KEY_VALUE_HEADS, HEAD_WIDTH)
    value_head_rows = value_reduced.reshape(
        batch_count, SEQUENCE_LENGTH, KEY_VALUE_HEADS, HEAD_WIDTH
    )
    scores = attention_scores(query_head_rows, key_head_rows, SEQUENCE_LENGTH)
    row_top = jnp.max(scores, axis=-1, keepdims=True)
    unscaled = jnp.exp(scores - row_top)
    row_total = jnp.sum(unscaled, axis=-1, keepdims=True)
    shares = unscaled / row_total
    log_total = row_top + jnp.log(row_total)
    context = jnp.einsum(
        "bkjqs,bskd->bqkjd",
        shares.astype(REDUCED_DTYPE),
        value_head_rows,
        preferred_element_type=WIDER,
    )
    context_low = context.reshape(token_rows, QUERY_HEADS * HEAD_WIDTH).astype(REDUCED_DTYPE)
    attend_term = matmul(context_low, gathered[14])
    middle = inputs + mixer_term + attend_term
    norm_two, norm_two_back = jax.vjp(rms_scale, middle, gathered[15].astype(WIDER))
    normed_two = norm_two.astype(REDUCED_DTYPE)
    gate_value = matmul(normed_two, gathered[16])
    up_value = matmul(normed_two, gathered[17])
    activated, swiglu_back = jax.vjp(swiglu, gate_value, up_value)
    activated_low = activated.astype(REDUCED_DTYPE)
    output = (middle + matmul(activated_low, gathered[18])).astype(REDUCED_DTYPE)
    later_half = (
        lax.all_gather(first_gain, "shard", axis=0, tiled=True),
        lax.all_gather(mixer_gate, "shard", axis=0, tiled=True),
        lax.all_gather(mixer_input, "shard", axis=0, tiled=True),
        lax.all_gather(step_weight, "shard", axis=0, tiled=True),
        lax.all_gather(conv_weight, "shard", axis=1, tiled=True),
        lax.all_gather(conv_bias, "shard", axis=0, tiled=True),
        lax.all_gather(step_bias, "shard", axis=0, tiled=True),
        lax.all_gather(decay_log, "shard", axis=0, tiled=True),
        lax.all_gather(skip_weight, "shard", axis=0, tiled=True),
        lax.all_gather(mixer_gain, "shard", axis=0, tiled=True),
        lax.all_gather(mixer_output, "shard", axis=0, tiled=True),
        lax.all_gather(query_matrix, "shard", axis=0, tiled=True),
        lax.all_gather(key_matrix, "shard", axis=0, tiled=True),
        lax.all_gather(value_matrix, "shard", axis=0, tiled=True),
        lax.all_gather(attn_output, "shard", axis=0, tiled=True),
        lax.all_gather(second_gain, "shard", axis=0, tiled=True),
        lax.all_gather(ffn_gate, "shard", axis=0, tiled=True),
        lax.all_gather(ffn_up, "shard", axis=0, tiled=True),
        lax.all_gather(ffn_down, "shard", axis=0, tiled=True),
    )
    grad_activated = input_gradient(cotangent, later_half[18])
    grad_gate_wide, grad_up_wide = swiglu_back(grad_activated)
    grad_gate_low = grad_gate_wide.astype(REDUCED_DTYPE)
    grad_up_low = grad_up_wide.astype(REDUCED_DTYPE)
    grad_normed_two = input_gradient(grad_gate_low, later_half[16]) + input_gradient(
        grad_up_low, later_half[17]
    )
    grad_middle_norm, grad_gain_two = norm_two_back(grad_normed_two)
    grad_middle = cotangent.astype(WIDER) + grad_middle_norm
    branch_gradient = grad_middle.astype(REDUCED_DTYPE)
    grad_context = (
        input_gradient(branch_gradient, later_half[14])
        .astype(REDUCED_DTYPE)
        .reshape(batch_count, SEQUENCE_LENGTH, KEY_VALUE_HEADS, shard_groups, HEAD_WIDTH)
    )
    shares_again = jnp.exp(
        attention_scores(query_head_rows, key_head_rows, SEQUENCE_LENGTH) - log_total
    )
    grad_shares = jnp.einsum(
        "bqkjd,bskd->bkjqs", grad_context, value_head_rows, preferred_element_type=WIDER
    )
    value_gradient_full = jnp.einsum(
        "bkjqs,bqkjd->bskd",
        shares_again.astype(REDUCED_DTYPE),
        grad_context,
        preferred_element_type=WIDER,
    )
    grad_scores = shares_again * (
        grad_shares - jnp.sum(shares_again * grad_shares, axis=-1, keepdims=True)
    )
    grad_raw = (grad_scores * HEAD_WIDTH ** (-0.5)).astype(REDUCED_DTYPE)
    grad_query_wide = jnp.einsum(
        "bkjqs,bskd->bqkjd", grad_raw, key_head_rows, preferred_element_type=WIDER
    )
    key_gradient_full = jnp.einsum(
        "bkjqs,bqkjd->bskd", grad_raw, query_head_rows, preferred_element_type=WIDER
    )
    query_grad_low = grad_query_wide.reshape(token_rows, QUERY_HEADS * HEAD_WIDTH).astype(
        REDUCED_DTYPE
    )
    key_gradient_reduced = key_gradient_full.reshape(
        token_rows, KEY_VALUE_HEADS * HEAD_WIDTH
    ).astype(REDUCED_DTYPE)
    value_gradient_reduced = value_gradient_full.reshape(
        token_rows, KEY_VALUE_HEADS * HEAD_WIDTH
    ).astype(REDUCED_DTYPE)
    grad_mixer_norm = input_gradient(branch_gradient, later_half[10])
    (
        grad_gate_in,
        grad_mixed_in,
        grad_step_in,
        grad_taps,
        grad_offset,
        grad_step_offset,
        grad_decay,
        grad_skip,
        grad_gain_mixer,
    ) = mixer_back(grad_mixer_norm)
    gate_in_low = grad_gate_in.astype(REDUCED_DTYPE)
    mixed_in_low = grad_mixed_in.astype(REDUCED_DTYPE)
    step_in_low = grad_step_in.astype(REDUCED_DTYPE)
    grad_normed = (
        input_gradient(query_grad_low, later_half[11])
        + input_gradient(key_gradient_reduced, later_half[12])
        + input_gradient(value_gradient_reduced, later_half[13])
        + input_gradient(gate_in_low, later_half[1])
        + input_gradient(mixed_in_low, later_half[2])
        + input_gradient(step_in_low, later_half[3])
    )
    grad_inputs_norm, grad_gain_one = norm_one_back(grad_normed)
    tokens_grad = (grad_middle + grad_inputs_norm).astype(REDUCED_DTYPE)
    grad_down = weight_grad(activated_low, cotangent)
    grad_gate_ffn = weight_grad(normed_two, grad_gate_low)
    grad_up_ffn = weight_grad(normed_two, grad_up_low)
    grad_attend = weight_grad(context_low, branch_gradient)
    grad_mixer_proj = weight_grad(mixer_norm, branch_gradient)
    grad_query = weight_grad(normalized_input, query_grad_low)
    grad_key = weight_grad(normalized_input, key_gradient_reduced)
    grad_value = weight_grad(normalized_input, value_gradient_reduced)
    grad_gate_proj = weight_grad(normalized_input, gate_in_low)
    grad_input_proj = weight_grad(normalized_input, mixed_in_low)
    grad_step_proj = weight_grad(normalized_input, step_in_low)
    owned = (
        lax.psum_scatter(
            grad_gain_one.astype(jnp.bfloat16), "shard", scatter_dimension=0, tiled=True
        ).astype(jnp.float32),
        lax.psum_scatter(
            grad_gate_proj.astype(jnp.bfloat16), "shard", scatter_dimension=0, tiled=True
        ).astype(jnp.float32),
        lax.psum_scatter(
            grad_input_proj.astype(jnp.bfloat16), "shard", scatter_dimension=0, tiled=True
        ).astype(jnp.float32),
        lax.psum_scatter(
            grad_step_proj.astype(jnp.bfloat16), "shard", scatter_dimension=0, tiled=True
        ).astype(jnp.float32),
        lax.psum_scatter(
            grad_taps.astype(jnp.bfloat16), "shard", scatter_dimension=1, tiled=True
        ).astype(jnp.float32),
        lax.psum_scatter(
            grad_offset.astype(jnp.bfloat16), "shard", scatter_dimension=0, tiled=True
        ).astype(jnp.float32),
        lax.psum_scatter(
            grad_step_offset.astype(jnp.bfloat16), "shard", scatter_dimension=0, tiled=True
        ).astype(jnp.float32),
        lax.psum_scatter(
            grad_decay.astype(jnp.bfloat16), "shard", scatter_dimension=0, tiled=True
        ).astype(jnp.float32),
        lax.psum_scatter(
            grad_skip.astype(jnp.bfloat16), "shard", scatter_dimension=0, tiled=True
        ).astype(jnp.float32),
        lax.psum_scatter(
            grad_gain_mixer.astype(jnp.bfloat16), "shard", scatter_dimension=0, tiled=True
        ).astype(jnp.float32),
        lax.psum_scatter(
            grad_mixer_proj.astype(jnp.bfloat16), "shard", scatter_dimension=0, tiled=True
        ).astype(jnp.float32),
        lax.psum_scatter(
            grad_query.astype(jnp.bfloat16), "shard", scatter_dimension=0, tiled=True
        ).astype(jnp.float32),
        lax.psum_scatter(
            grad_key.astype(jnp.bfloat16), "shard", scatter_dimension=0, tiled=True
        ).astype(jnp.float32),
        lax.psum_scatter(
            grad_value.astype(jnp.bfloat16), "shard", scatter_dimension=0, tiled=True
        ).astype(jnp.float32),
        lax.psum_scatter(
            grad_attend.astype(jnp.bfloat16), "shard", scatter_dimension=0, tiled=True
        ).astype(jnp.float32),
        lax.psum_scatter(
            grad_gain_two.astype(jnp.bfloat16), "shard", scatter_dimension=0, tiled=True
        ).astype(jnp.float32),
        lax.psum_scatter(
            grad_gate_ffn.astype(jnp.bfloat16), "shard", scatter_dimension=0, tiled=True
        ).astype(jnp.float32),
        lax.psum_scatter(
            grad_up_ffn.astype(jnp.bfloat16), "shard", scatter_dimension=0, tiled=True
        ).astype(jnp.float32),
        lax.psum_scatter(
            grad_down.astype(jnp.bfloat16), "shard", scatter_dimension=0, tiled=True
        ).astype(jnp.float32),
    )
    spread_all = (
        lax.psum_scatter(owned[0], "rep", scatter_dimension=0, tiled=True),
        lax.psum_scatter(owned[1], "rep", scatter_dimension=0, tiled=True),
        lax.psum_scatter(owned[2], "rep", scatter_dimension=0, tiled=True),
        lax.psum_scatter(owned[3], "rep", scatter_dimension=0, tiled=True),
        lax.psum_scatter(owned[4], "rep", scatter_dimension=1, tiled=True),
        lax.psum_scatter(owned[5], "rep", scatter_dimension=0, tiled=True),
        lax.psum_scatter(owned[9], "rep", scatter_dimension=0, tiled=True),
        lax.psum_scatter(owned[10], "rep", scatter_dimension=0, tiled=True),
        lax.psum_scatter(owned[11], "rep", scatter_dimension=0, tiled=True),
        lax.psum_scatter(owned[12], "rep", scatter_dimension=0, tiled=True),
        lax.psum_scatter(owned[13], "rep", scatter_dimension=0, tiled=True),
        lax.psum_scatter(owned[14], "rep", scatter_dimension=0, tiled=True),
        lax.psum_scatter(owned[15], "rep", scatter_dimension=0, tiled=True),
        lax.psum_scatter(owned[16], "rep", scatter_dimension=0, tiled=True),
        lax.psum_scatter(owned[17], "rep", scatter_dimension=0, tiled=True),
        lax.psum_scatter(owned[18], "rep", scatter_dimension=0, tiled=True),
    )
    heads = lax.psum((owned[6], owned[7], owned[8]), "rep")
    finals = tuple(spread_all[0:6]) + tuple(heads) + tuple(spread_all[6:16])
    return (output, tokens_grad) + tuple(finals)


def solution(mesh):
    placed = (
        P(("shard", "rep"), None),
        P(("shard", "rep"), None),
        P("shard"),
        P("shard", None),
        P("shard", None),
        P("shard", None),
        P(None, "shard"),
        P("shard"),
        P("shard"),
        P("shard"),
        P("shard"),
        P("shard"),
        P("shard", None),
        P("shard", None),
        P("shard", None),
        P("shard", None),
        P("shard", None),
        P("shard"),
        P("shard", None),
        P("shard", None),
        P("shard", None),
    )
    return jax.shard_map(
        local,
        mesh=mesh,
        in_specs=placed,
        out_specs=(
            P(("shard", "rep"), None),
            P(("shard", "rep"), None),
            P(("shard", "rep")),
            P(("shard", "rep"), None),
            P(("shard", "rep"), None),
            P(("shard", "rep"), None),
            P(None, ("shard", "rep")),
            P(("shard", "rep")),
            P("shard"),
            P("shard"),
            P("shard"),
            P(("shard", "rep")),
            P(("shard", "rep"), None),
            P(("shard", "rep"), None),
            P(("shard", "rep"), None),
            P(("shard", "rep"), None),
            P(("shard", "rep"), None),
            P(("shard", "rep")),
            P(("shard", "rep"), None),
            P(("shard", "rep"), None),
            P(("shard", "rep"), None),
        ),
        check_vma=False,
    )
```

profile of v0, /device:TPU:0, one launch (start us, length us, event | category | flops | bytes accessed | tf_op | source)
XLA Modules:
  0.0 1450.7 jit_solution(10154875200587894231)
XLA Ops:
  15.4 6.0 all-gather.3
  27.8 7.4 all-reduce.30
  52.6 7.6 all_gather.80
  60.3 6.0 all_gather.79
  84.5 9.7 all-gather.15.cloned.1.call-done
  97.9 26.3 %all-gather.17.cloned.1.call-done = bf16[1536,1024]{1,0:T(8,128)(2,1)} async-done(((bf16[384,1024]{1,0:T(8,128)(2,1)}), bf16[1536,1024]{1,0:T(8,128)(2,1)}) %all-gather.17.cloned.1.call-update) | async-done | bytes 3145744 | tf_op jit(solution)/shard_map/all_gather | solution.py:123
  126.8 15.6 %all-gather.21.cloned.1.call-done = bf16[512,1024]{1,0:T(8,128)(2,1)} async-done(((bf16[128,1024]{1,0:T(8,128)(2,1)}), bf16[512,1024]{1,0:T(8,128)(2,1)}) %all-gather.21.cloned.1.call-update) | async-done | bytes 1048592 | tf_op jit(solution)/shard_map/all_gather | solution.py:127
  144.8 33.6 %all-gather.25.cloned.1.call-done = bf16[1024,2048]{1,0:T(8,128)(2,1)} async-done(((bf16[256,2048]{1,0:T(8,128)(2,1)}), bf16[1024,2048]{1,0:T(8,128)(2,1)}) %all-gather.25.cloned.1.call-update) | async-done | bytes 4194320 | tf_op jit(solution)/shard_map/all_gather | solution.py:130
  182.2 32.2 %all-gather.23.cloned.1.call-done = bf16[1024,2048]{1,0:T(8,128)(2,1)} async-done(((bf16[256,2048]{1,0:T(8,128)(2,1)}), bf16[1024,2048]{1,0:T(8,128)(2,1)}) %all-gather.23.cloned.1.call-update) | async-done | bytes 4194320 | tf_op jit(solution)/shard_map/all_gather | solution.py:129
  218.3 32.2 %all-gather.27.cloned.1.call-done = bf16[2048,1024]{1,0:T(8,128)(2,1)} async-done(((bf16[512,1024]{1,0:T(8,128)(2,1)}), bf16[2048,1024]{1,0:T(8,128)(2,1)}) %all-gather.27.cloned.1.call-update) | async-done | bytes 4194320 | tf_op jit(solution)/shard_map/all_gather | solution.py:131
  346.3 12.7 reduce-scatter.47.cloned.1.call-done
  360.5 25.9 %reduce-scatter.43.cloned.1.call-done = bf16[256,512]{1,0:T(8,128)(2,1)} async-done(((bf16[1024,512]{1,0:T(8,128)(2,1)}), bf16[256,512]{1,0:T(8,128)(2,1)}) %reduce-scatter.43.cloned.1.call-update) | async-done | bytes 262160 | tf_op jit(solution)/shard_map/reduce_scatter | solution.py:350
  388.3 25.6 %reduce-scatter.55.cloned.1.call-done = bf16[128,1024]{1,0:T(8,128)(2,1)} async-done(((bf16[512,1024]{1,0:T(8,128)(2,1)}), bf16[128,1024]{1,0:T(8,128)(2,1)}) %reduce-scatter.55.cloned.1.call-update) | async-done | bytes 262160 | tf_op jit(solution)/shard_map/reduce_scatter | solution.py:359
  415.8 38.7 %reduce-scatter.39.cloned.1.call-done = bf16[384,1024]{1,0:T(8,128)(2,1)} async-done(((bf16[1536,1024]{1,0:T(8,128)(2,1)}), bf16[384,1024]{1,0:T(8,128)(2,1)}) %reduce-scatter.39.cloned.1.call-update) | async-done | bytes 786448 | tf_op jit(solution)/shard_map/reduce_scatter | solution.py:347
  457.0 37.8 %reduce-scatter.29.cloned.1.call-done = bf16[256,1536]{1,0:T(8,128)(2,1)} async-done(((bf16[1024,1536]{1,0:T(8,128)(2,1)}), bf16[256,1536]{1,0:T(8,128)(2,1)}) %reduce-scatter.29.cloned.1.call-update) | async-done | bytes 786448 | tf_op jit(solution)/shard_map/reduce_scatter | solution.py:320
  497.4 41.2 %reduce-scatter.33.cloned.1.call-done = bf16[256,1792]{1,0:T(8,128)(2,1)} async-done(((bf16[1024,1792]{1,0:T(8,128)(2,1)}), bf16[256,1792]{1,0:T(8,128)(2,1)}) %reduce-scatter.33.cloned.1.call-update) | async-done | bytes 917520 | tf_op jit(solution)/shard_map/reduce_scatter | solution.py:323
  541.3 44.3 %reduce-scatter.67.cloned.1.call-done = bf16[512,1024]{1,0:T(8,128)(2,1)} async-done(((bf16[2048,1024]{1,0:T(8,128)(2,1)}), bf16[512,1024]{1,0:T(8,128)(2,1)}) %reduce-scatter.67.cloned.1.call-update) | async-done | bytes 1048592 | tf_op jit(solution)/shard_map/reduce_scatter | solution.py:371
  588.4 44.2 %reduce-scatter.63.cloned.1.call-done = bf16[256,2048]{1,0:T(8,128)(2,1)} async-done(((bf16[1024,2048]{1,0:T(8,128)(2,1)}), bf16[256,2048]{1,0:T(8,128)(2,1)}) %reduce-scatter.63.cloned.1.call-update) | async-done | bytes 1048592 | tf_op jit(solution)/shard_map/reduce_scatter | solution.py:368
  635.8 43.9 %reduce-scatter.59.cloned.1.call-done = bf16[256,2048]{1,0:T(8,128)(2,1)} async-done(((bf16[1024,2048]{1,0:T(8,128)(2,1)}), bf16[256,2048]{1,0:T(8,128)(2,1)}) %reduce-scatter.59.cloned.1.call-update) | async-done | bytes 1048592 | tf_op jit(solution)/shard_map/reduce_scatter | solution.py:365
  696.9 10.6 all-reduce.29
  713.5 37.6 %all-reduce.28 = (f32[256]{0:T(256)S(1)}, f32[4,448]{1,0:T(4,128)S(1)}, f32[448]{0:T(512)S(1)}, f32[6]{0:T(128)}, f32[6]{0:T(128)}, /*index=5*/f32[6]{0:T(128)}, f32[384]{0:T(512)S(1)}, f32[256]{0:T(256)S(1)}) all-reduce(f32[256]{0:T(256)S(1)} %get-tuple-element.92, ...), channel_id=3, replica_groups=mesh['shard'=4,'rep'=8] {'rep'}, use_global_device_ids=true, to_apply=%region_17.18.clone | all-reduce | flops 3154 | bytes 21648
  754.1 14.1 reduce-scatter.71.cloned.1.call-done
  769.5 62.8 %reduce-scatter.53.cloned.1.call-done = f32[32,128]{1,0:T(8,128)} async-done(((f32[256,128]{1,0:T(8,128)}), f32[32,128]{1,0:T(8,128)}) %reduce-scatter.53.cloned.1.call-update) | async-done | bytes 16400 | tf_op jit(solution)/shard_map/reduce_scatter | solution.py:386
  832.3 64.2 %reduce-scatter.49.cloned.1.call-done = f32[32,128]{1,0:T(8,128)} async-done(((f32[256,128]{1,0:T(8,128)}), f32[32,128]{1,0:T(8,128)}) %reduce-scatter.49.cloned.1.call-update) | async-done | bytes 16400 | tf_op jit(solution)/shard_map/reduce_scatter | solution.py:385
  896.5 65.1 %reduce-scatter.45.cloned.1.call-done = f32[32,512]{1,0:T(8,128)} async-done(((f32[256,512]{1,0:T(8,128)}), f32[32,512]{1,0:T(8,128)}) %reduce-scatter.45.cloned.1.call-update) | async-done | bytes 65552 | tf_op jit(solution)/shard_map/reduce_scatter | solution.py:384
  961.6 64.9 %reduce-scatter.57.cloned.1.call-done = f32[16,1024]{1,0:T(8,128)} async-done(((f32[128,1024]{1,0:T(8,128)}), f32[16,1024]{1,0:T(8,128)}) %reduce-scatter.57.cloned.1.call-update) | async-done | bytes 65552 | tf_op jit(solution)/shard_map/reduce_scatter | solution.py:387
  1026.5 68.1 %reduce-scatter.41.cloned.1.call-done = f32[48,1024]{1,0:T(8,128)} async-done(((f32[384,1024]{1,0:T(8,128)}), f32[48,1024]{1,0:T(8,128)}) %reduce-scatter.41.cloned.1.call-update) | async-done | bytes 196624 | tf_op jit(solution)/shard_map/reduce_scatter | solution.py:383
  1094.6 67.7 %reduce-scatter.31.cloned.1.call-done = f32[32,1536]{1,0:T(8,128)} async-done(((f32[256,1536]{1,0:T(8,128)}), f32[32,1536]{1,0:T(8,128)}) %reduce-scatter.31.cloned.1.call-update) | async-done | bytes 196624 | tf_op jit(solution)/shard_map/reduce_scatter | solution.py:377
  1162.3 69.6 %reduce-scatter.35.cloned.1.call-done = f32[32,1792]{1,0:T(8,128)} async-done(((f32[256,1792]{1,0:T(8,128)}), f32[32,1792]{1,0:T(8,128)}) %reduce-scatter.35.cloned.1.call-update) | async-done | bytes 229392 | tf_op jit(solution)/shard_map/reduce_scatter | solution.py:378
  1231.9 70.5 %reduce-scatter.69.cloned.1.call-done = f32[64,1024]{1,0:T(8,128)} async-done(((f32[512,1024]{1,0:T(8,128)}), f32[64,1024]{1,0:T(8,128)}) %reduce-scatter.69.cloned.1.call-update) | async-done | bytes 262160 | tf_op jit(solution)/shard_map/reduce_scatter | solution.py:391
  1302.4 70.6 %reduce-scatter.65.cloned.1.call-done = f32[32,2048]{1,0:T(8,128)} async-done(((f32[256,2048]{1,0:T(8,128)}), f32[32,2048]{1,0:T(8,128)}) %reduce-scatter.65.cloned.1.call-update) | async-done | bytes 262160 | tf_op jit(solution)/shard_map/reduce_scatter | solution.py:390
  1373.0 70.7 %reduce-scatter.61.cloned.1.call-done = f32[32,2048]{1,0:T(8,128)} async-done(((f32[256,2048]{1,0:T(8,128)}), f32[32,2048]{1,0:T(8,128)}) %reduce-scatter.61.cloned.1.call-update) | async-done | bytes 262160 | tf_op jit(solution)/shard_map/reduce_scatter | solution.py:389
  (400 shorter events, 201.5 us)
Async XLA Ops:
  7.2 59.9 %all-gather.19.cloned.1.call-start = ((), (), s32[]{:S(2)}) async-start(), calls=%async_computation.26 | async-start | bytes 1310720 | tf_op jit(solution)/shard_map/all_gather | solution.py:124
  8.0 62.6 %all-gather.13.cloned.1.call-start = ((), (), s32[]{:S(2)}) async-start(), calls=%async_computation.23 | async-start | bytes 4587520 | tf_op jit(solution)/shard_map/all_gather | solution.py:115
  8.8 85.4 %all-gather.15.cloned.1.call-start = ((), (), s32[]{:S(2)}) async-start(), calls=%async_computation.24 | async-start | bytes 3932160 | tf_op jit(solution)/shard_map/all_gather | solution.py:114
  9.5 114.7 %all-gather.17.cloned.1.call-start = ((), (), s32[]{:S(2)}) async-start(), calls=%async_computation.25 | async-start | bytes 3932160 | tf_op jit(solution)/shard_map/all_gather | solution.py:123
  10.1 132.3 %all-gather.21.cloned.1.call-start = ((), (), s32[]{:S(2)}) async-start(), calls=%async_computation.27 | async-start | bytes 1310720 | tf_op jit(solution)/shard_map/all_gather | solution.py:127
  10.7 167.6 %all-gather.25.cloned.1.call-start = ((), (), s32[]{:S(2)}) async-start(), calls=%async_computation.29 | async-start | bytes 5242880 | tf_op jit(solution)/shard_map/all_gather | solution.py:130
  11.3 203.1 %all-gather.23.cloned.1.call-start = ((), (), s32[]{:S(2)}) async-start(), calls=%async_computation.28 | async-start | bytes 5242880 | tf_op jit(solution)/shard_map/all_gather | solution.py:129
  12.0 238.4 %all-gather.27.cloned.1.call-start = ((), (), s32[]{:S(2)}) async-start(), calls=%async_computation.30 | async-start | bytes 5242880 | tf_op jit(solution)/shard_map/all_gather | solution.py:131
  12.8 330.3 %reduce-scatter.37.cloned.1.call-start = ((), (), s32[]{:S(2)}) async-start(), calls=%async_computation.35 | async-start | bytes 61440 | tf_op jit(solution)/shard_map/reduce_scatter | solution.py:326
  15.4 78.9 %copy-start.49 = (f32[128]{0:T(128)}, f32[128]{0:T(128)S(1)}, u32[]{:S(2)}) copy-start(f32[128]{0:T(128)S(1)} %fusion.67) | copy-start | bytes 1540
  293.2 51.5 %reduce-scatter.51.cloned.1.call-start = ((), (), s32[]{:S(2)}) async-start(), calls=%async_computation.42 | async-start | bytes 327680 | tf_op jit(solution)/shard_map/reduce_scatter | solution.py:356
  295.8 63.2 %reduce-scatter.47.cloned.1.call-start = ((), (), s32[]{:S(2)}) async-start(), calls=%async_computation.40 | async-start | bytes 327680 | tf_op jit(solution)/shard_map/reduce_scatter | solution.py:353
  300.7 85.8 %reduce-scatter.43.cloned.1.call-start = ((), (), s32[]{:S(2)}) async-start(), calls=%async_computation.38 | async-start | bytes 1310720 | tf_op jit(solution)/shard_map/reduce_scatter | solution.py:350
  304.1 109.8 %reduce-scatter.55.cloned.1.call-start = ((), (), s32[]{:S(2)}) async-start(), calls=%async_computation.44 | async-start | bytes 1310720 | tf_op jit(solution)/shard_map/reduce_scatter | solution.py:359
  305.6 148.8 %reduce-scatter.39.cloned.1.call-start = ((), (), s32[]{:S(2)}) async-start(), calls=%async_computation.36 | async-start | bytes 3932160 | tf_op jit(solution)/shard_map/reduce_scatter | solution.py:347
  308.5 186.3 %reduce-scatter.29.cloned.1.call-start = ((), (), s32[]{:S(2)}) async-start(), calls=%async_computation.31 | async-start | bytes 3932160 | tf_op jit(solution)/shard_map/reduce_scatter | solution.py:320
  313.5 225.1 %reduce-scatter.33.cloned.1.call-start = ((), (), s32[]{:S(2)}) async-start(), calls=%async_computation.33 | async-start | bytes 4587520 | tf_op jit(solution)/shard_map/reduce_scatter | solution.py:323
  328.9 256.7 %reduce-scatter.67.cloned.1.call-start = ((), (), s32[]{:S(2)}) async-start(), calls=%async_computation.50 | async-start | bytes 5242880 | tf_op jit(solution)/shard_map/reduce_scatter | solution.py:371
  333.2 299.4 %reduce-scatter.63.cloned.1.call-start = ((), (), s32[]{:S(2)}) async-start(), calls=%async_computation.48 | async-start | bytes 5242880 | tf_op jit(solution)/shard_map/reduce_scatter | solution.py:368
  337.5 342.2 %reduce-scatter.59.cloned.1.call-start = ((), (), s32[]{:S(2)}) async-start(), calls=%async_computation.46 | async-start | bytes 5242880 | tf_op jit(solution)/shard_map/reduce_scatter | solution.py:365
  341.9 370.6 %reduce-scatter.73.cloned.1.call-start = ((), (), s32[]{:S(2)}) async-start(), calls=%async_computation.53 | async-start | bytes 573440
  343.1 425.1 %reduce-scatter.71.cloned.1.call-start = ((), (), s32[]{:S(2)}) async-start(), calls=%async_computation.52 | async-start | bytes 147456
  344.6 487.7 %reduce-scatter.53.cloned.1.call-start = ((), (), s32[]{:S(2)}) async-start(), calls=%async_computation.43 | async-start | bytes 147456 | tf_op jit(solution)/shard_map/reduce_scatter | solution.py:386
  346.2 550.2 %reduce-scatter.49.cloned.1.call-start = ((), (), s32[]{:S(2)}) async-start(), calls=%async_computation.41 | async-start | bytes 147456 | tf_op jit(solution)/shard_map/reduce_scatter | solution.py:385
  360.5 601.1 %reduce-scatter.45.cloned.1.call-start = ((), (), s32[]{:S(2)}) async-start(), calls=%async_computation.39 | async-start | bytes 589824 | tf_op jit(solution)/shard_map/reduce_scatter | solution.py:384
  388.3 638.2 %reduce-scatter.57.cloned.1.call-start = ((), (), s32[]{:S(2)}) async-start(), calls=%async_computation.45 | async-start | bytes 589824 | tf_op jit(solution)/shard_map/reduce_scatter | solution.py:387
  415.7 678.9 %reduce-scatter.41.cloned.1.call-start = ((), (), s32[]{:S(2)}) async-start(), calls=%async_computation.37 | async-start | bytes 1769472 | tf_op jit(solution)/shard_map/reduce_scatter | solution.py:383
  456.9 705.3 %reduce-scatter.31.cloned.1.call-start = ((), (), s32[]{:S(2)}) async-start(), calls=%async_computation.32 | async-start | bytes 1769472 | tf_op jit(solution)/shard_map/reduce_scatter | solution.py:377
  497.4 734.5 %reduce-scatter.35.cloned.1.call-start = ((), (), s32[]{:S(2)}) async-start(), calls=%async_computation.34 | async-start | bytes 2064384 | tf_op jit(solution)/shard_map/reduce_scatter | solution.py:378
  541.2 761.2 %reduce-scatter.69.cloned.1.call-start = ((), (), s32[]{:S(2)}) async-start(), calls=%async_computation.51 | async-start | bytes 2359296 | tf_op jit(solution)/shard_map/reduce_scatter | solution.py:391
  588.4 784.6 %reduce-scatter.65.cloned.1.call-start = ((), (), s32[]{:S(2)}) async-start(), calls=%async_computation.49 | async-start | bytes 2359296 | tf_op jit(solution)/shard_map/reduce_scatter | solution.py:390
  635.6 808.1 %reduce-scatter.61.cloned.1.call-start = ((), (), s32[]{:S(2)}) async-start(), calls=%async_computation.47 | async-start | bytes 2359296 | tf_op jit(solution)/shard_map/reduce_scatter | solution.py:389
  (95 other events, 1197.4 us)
Sparse Core Ops, SparseCore 0:
  9.6 19.4 all-gather.18
  30.7 33.2 all-gather.12
  65.6 28.5 all-gather.14
  95.6 28.5 all-gather.16
  125.6 16.7 all-gather.20
  143.8 34.4 all-gather.24
  179.9 34.4 all-gather.22
  216.0 34.4 all-gather.26
  293.3 19.4 reduce-scatter.36
  315.8 19.9 reduce-scatter.50
  338.9 20.0 reduce-scatter.46
  361.5 24.8 reduce-scatter.42
  388.9 24.8 reduce-scatter.54
  416.4 37.9 reduce-scatter.38
  456.8 37.9 reduce-scatter.28
  497.4 41.2 reduce-scatter.32
  541.0 44.4 reduce-scatter.66
  588.1 44.5 reduce-scatter.62
  635.2 44.4 reduce-scatter.58
  682.2 21.3 reduce-scatter.72
  707.3 60.8 reduce-scatter.70
  772.4 59.8 reduce-scatter.52
  836.6 59.8 reduce-scatter.48
  900.6 60.9 reduce-scatter.44
  965.5 60.9 reduce-scatter.56
  1030.7 63.8 reduce-scatter.40
  1098.4 63.7 reduce-scatter.30
  1166.7 65.1 reduce-scatter.34
  1236.0 66.3 reduce-scatter.68
  1306.3 66.5 reduce-scatter.64
  1377.1 66.5 reduce-scatter.60
where the time goes:
time: 1460 us; the launch traced here: 1450 us
  waiting for transfers between devices  1160 us (79%)
  blocking collectives  96.3 us (7%)
  matrix products  95.4 us (7%)
  other arithmetic  44.9 us (3%)
  local copies, waits for them, and re-layouts  32.7 us (2%)
  between operations  21.8 us (1%)
    reduce_scatter x1, waiting for transfers between devices, local(): lax.psum_scatter(owned[16], 'rep', scatter_dimension=0, tiled=True)  70.7 us
    reduce_scatter x1, waiting for transfers between devices, local(): lax.psum_scatter(owned[17], 'rep', scatter_dimension=0, tiled=True)  70.6 us
    reduce_scatter x1, waiting for transfers between devices, local(): lax.psum_scatter(owned[18], 'rep', scatter_dimension=0, tiled=True)  70.5 us
    reduce_scatter x1, waiting for transfers between devices, local(): lax.psum_scatter(owned[2], 'rep', scatter_dimension=0, tiled=True)  69.6 us
    reduce_scatter x1, waiting for transfers between devices, local(): lax.psum_scatter(owned[10], 'rep', scatter_dimension=0, tiled=True)  68.1 us
    reduce_scatter x1, waiting for transfers between devices, local(): lax.psum_scatter(owned[1], 'rep', scatter_dimension=0, tiled=True)  67.7 us
    reduce_scatter x1, waiting for transfers between devices, local(): lax.psum_scatter(owned[11], 'rep', scatter_dimension=0, tiled=True)  65.1 us
    reduce_scatter x1, waiting for transfers between devices, local(): lax.psum_scatter(owned[14], 'rep', scatter_dimension=0, tiled=True)  64.9 us
  transfers between devices with their start and end apart: 31, of which 26 were waited for; matrix products, arithmetic and copies ran while one was open for 9% of the time, Pallas kernels for 0%

commit v1 on v0

v1 whole, which is shorter than its diff:
```python
import jax
import jax.numpy as jnp
from jax import lax
from jax.experimental import pallas as pl
from jax.experimental.pallas import tpu as pltpu
from jax.sharding import PartitionSpec as P

QUERY_HEADS = 8
KEY_VALUE_HEADS = 2
HEAD_WIDTH = 64
HM = 24
P_SIZE = 64
N = 128
KC = 4
SEQUENCE_LENGTH = 128
DS = 1536
XBC = 1792
WIDTH = 1024
QW = QUERY_HEADS * HEAD_WIDTH
KW = KEY_VALUE_HEADS * HEAD_WIDTH
GATE_AT, MIXED_AT = 0, DS
Q_AT = MIXED_AT + XBC
K_AT = Q_AT + QW
V_AT = K_AT + KW
STEP_AT = V_AT + KW
IN_COLS = STEP_AT + 128


EPS = 1e-05
HIGH = lax.Precision.HIGHEST
BF = jnp.bfloat16
F32 = jnp.float32


def rms_scale(values, gain):
    return values * lax.rsqrt(jnp.mean(values * values, axis=-1, keepdims=True) + EPS) * gain


def swiglu(gate_value, up_value):
    return jax.nn.silu(gate_value) * up_value


def mixer_core(
    gate_in,
    mixed_in,
    step_in,
    kernel_taps,
    kernel_offset,
    step_offset,
    decay_rates,
    skip_scale,
    norm_gain,
):
    batch_count, token_length = (mixed_in.shape[0], mixed_in.shape[1])
    padded = jnp.pad(mixed_in, ((0, 0), (KC - 1, 0), (0, 0)))
    convolved = kernel_offset + padded[:, 0:token_length] * kernel_taps[0]
    for offset in range(1, KC):
        convolved = convolved + padded[:, offset : offset + token_length] * kernel_taps[offset]
    active = jax.nn.silu(convolved)
    inner_values = active[:, :, :DS].reshape(batch_count, token_length, HM, P_SIZE)
    in_state = active[:, :, DS : DS + N]
    out_state = active[:, :, DS + N :]
    step_size = jax.nn.softplus(step_in + step_offset)
    log_decay = -step_size * jnp.exp(decay_rates)
    running = jnp.cumsum(log_decay, axis=1)
    positions = jnp.arange(token_length)
    causal = (positions[:, None] >= positions[None, :])[None, :, :, None]
    spread = running[:, :, None, :] - running[:, None, :, :]
    decay_factor = jnp.where(causal, jnp.exp(jnp.where(causal, spread, 0.0)), 0.0)
    coupling = jnp.einsum("btn,bsn->bts", out_state, in_state, precision=HIGH)
    mixing = coupling[:, :, :, None] * decay_factor * step_size[:, None, :, :]
    result = (
        jnp.einsum("btsh,bshp->bthp", mixing, inner_values, precision=HIGH)
        + skip_scale[:, None] * inner_values
    )
    gated_values = result.reshape(batch_count, token_length, DS) * jax.nn.silu(gate_in)
    return rms_scale(gated_values, norm_gain)


def matmul(left, right):
    return jnp.dot(left, right, preferred_element_type=F32)


def weight_grad(left, grad):
    return lax.dot_general(left, grad, (((0,), (0,)), ((), ())), preferred_element_type=F32)


def input_gradient(grad, weight):
    return lax.dot_general(grad, weight, (((1,), (1,)), ((), ())), preferred_element_type=F32)


def attention_scores(query_head_rows, key_head_rows, token_length):
    positions = jnp.arange(token_length)
    causal = positions[:, None] >= positions[None, :]
    raw = jnp.einsum(
        "bqkjd,bskd->bkjqs", query_head_rows, key_head_rows, preferred_element_type=F32
    )
    return jnp.where(causal, raw * HEAD_WIDTH ** (-0.5), -1e30)


def swap(value, axis, bit):
    size = lax.axis_size(axis)
    return lax.ppermute(value, axis, [(i, i ^ bit) for i in range(size)])


def core(value):
    return swap(value, "shard", 1)


def over_x(value):
    return swap(value, "shard", 2)


def over_y(value):
    return swap(value, "rep", 1)


def over_z(value):
    return swap(value, "rep", 2)


def place_kernel(count, offsets, *refs):
    pieces, out, sems = refs[:count], refs[count], refs[count + 1]
    copies = []
    for i, piece in enumerate(pieces):
        rows = piece.shape[0]
        start = pl.multiple_of(offsets[i], rows)
        copies.append(
            pltpu.make_async_copy(piece, out.at[pl.ds(start, rows)], sems.at[i])
        )
    for copy in copies:
        copy.start()
    for copy in copies:
        copy.wait()


def place(pieces, offsets, rows):
    count = len(pieces)
    columns = pieces[0].shape[1]

    def body(*refs):
        place_kernel(count, *refs)

    any_spec = pl.BlockSpec(memory_space=pl.ANY)
    return pl.pallas_call(
        body,
        out_shape=jax.ShapeDtypeStruct((rows, columns), pieces[0].dtype),
        in_specs=[pl.BlockSpec(memory_space=pltpu.SMEM)] + [any_spec] * count,
        out_specs=any_spec,
        scratch_shapes=[pltpu.SemaphoreType.DMA((count,))],
        name="place",
        cost_estimate=pl.CostEstimate(
            flops=0, bytes_accessed=4 * rows * columns, transcendentals=0
        ),
    )(jnp.stack([jnp.asarray(o, jnp.int32) for o in offsets]), *pieces)


def gather_weight(weight, shard, rep, quick):
    rows = weight.shape[0]
    part = rows // 4
    mine = rep & 3

    def quarter(j):
        return lax.dynamic_slice_in_dim(weight, j * part, part, 0)

    near = core(weight)
    far_x = over_x(quarter(mine))
    far_y = over_y(far_x)
    far_z = over_z(far_x)
    if quick:
        last = [(over_x(quarter(mine ^ 3)), 0)]
    else:
        half = part // 2
        last = [(over_y(far_z[:half]), 0), (over_z(far_y[half:]), half)]
    far = [(far_x, mine * part), (far_y, (mine ^ 1) * part), (far_z, (mine ^ 2) * part)]
    far += [(value, (mine ^ 3) * part + at) for value, at in last]
    pieces = [(weight, shard * rows), (near, (shard ^ 1) * rows)]
    pieces += [(value, (shard ^ 2) * rows + at) for value, at in far]
    pieces += [(core(value), (shard ^ 3) * rows + at) for value, at in far]
    return place([p for p, _ in pieces], [o for _, o in pieces], 4 * rows)


def group_rows(value):
    far = over_x(value)
    return jnp.concatenate([value, core(value), far, core(far)], axis=0)


def group_columns(value, shard):
    tokens = value.shape[0]
    split = value.reshape(tokens, 4, -1)

    def pick(j):
        return lax.dynamic_index_in_dim(split, j, 1, keepdims=False)

    far = over_x(pick(shard ^ 2))
    beyond = core(over_x(pick(shard ^ 3)))
    return jnp.concatenate([pick(shard), core(pick(shard ^ 1)), far, beyond], axis=0)


def bit_of(index, bit):
    return (index // bit) & 1


def reduce_rep(columns, grads, rep):
    reps = lax.axis_size("rep")
    tokens = columns.shape[0]
    mine = bit_of(rep, 1)
    split = columns.reshape(tokens, reps // 2, 2, -1)

    def pick(j):
        return lax.dynamic_index_in_dim(split, j, 2, keepdims=False).reshape(tokens, -1)

    arrived = over_y(weight_grad(pick(1 - mine), grads).astype(BF))
    total = weight_grad(pick(mine), grads) + arrived.astype(F32)
    bit, left = 2, reps // 2
    while left > 1:
        total = total.reshape(left // 2, 2, -1, total.shape[-1])
        mine = bit_of(rep, bit)
        sent = lax.dynamic_index_in_dim(total, 1 - mine, 1, keepdims=False)
        arrived = swap(sent.astype(BF), "rep", bit)
        total = lax.dynamic_index_in_dim(total, mine, 1, keepdims=False) + arrived.astype(F32)
        bit, left = bit * 2, left // 2
    return total.reshape(-1, total.shape[-1])


def reduce_small(blocks, shard, rep):
    total = blocks
    for axis, index, bit in (("shard", shard, 2), ("shard", shard, 1)):
        mine = bit_of(index, bit)
        total = total.reshape((2, -1) + blocks.shape[1:])
        arrived = swap(
            lax.dynamic_index_in_dim(total, 1 - mine, 0, keepdims=False), axis, bit
        )
        total = lax.dynamic_index_in_dim(total, mine, 0, keepdims=False) + arrived
    total = total.reshape(blocks.shape[1:])
    bit = lax.axis_size("rep") // 2
    while bit:
        mine = bit_of(rep, bit)
        total = total.reshape(2, -1, total.shape[-1])
        arrived = swap(
            lax.dynamic_index_in_dim(total, 1 - mine, 0, keepdims=False), "rep", bit
        )
        total = lax.dynamic_index_in_dim(total, mine, 0, keepdims=False) + arrived
        bit //= 2
    return total.reshape(-1)


def local(
    tokens,
    cotangent,
    first_gain,
    mixer_gate,
    mixer_input,
    step_weight,
    conv_weight,
    conv_bias,
    step_bias,
    decay_log,
    skip_weight,
    mixer_gain,
    mixer_output,
    query_matrix,
    key_matrix,
    value_matrix,
    attn_output,
    second_gain,
    ffn_gate,
    ffn_up,
    ffn_down,
):
    shard = lax.axis_index("shard")
    rep = lax.axis_index("rep")
    reps = lax.axis_size("rep")

    small_parts = (
        first_gain,
        conv_weight.reshape(-1),
        conv_bias,
        step_bias,
        decay_log,
        skip_weight,
        mixer_gain,
        second_gain,
    )
    small = jnp.concatenate(small_parts)
    small = jnp.pad(small, (0, -small.shape[0] % 128)).reshape(1, -1)
    far_small = over_x(small)
    smalls = jnp.concatenate([small, core(small), far_small, core(far_small)], axis=0)
    smalls = jnp.take(smalls, jnp.arange(4) ^ shard, axis=0).astype(F32)
    full, at = [], 0
    for part in small_parts:
        full.append(smalls[:, at : at + part.shape[0]])
        at += part.shape[0]
    taps = full[1].reshape(4, KC, -1).transpose(1, 0, 2).reshape(KC, XBC)
    gain_one, offset, step_offset, decay_rates, skip_scale, gain_mixer, gain_two = (
        full[i].reshape(-1) for i in (0, 2, 3, 4, 5, 6, 7)
    )

    step_padded = jnp.pad(step_weight, ((0, 0), (0, IN_COLS - STEP_AT - HM)))
    in_shard = jnp.concatenate(
        [mixer_gate, mixer_input, query_matrix, key_matrix, value_matrix, step_padded], axis=1
    )
    w_in = gather_weight(in_shard, shard, rep, True)
    w_out = gather_weight(jnp.concatenate([mixer_output, attn_output], axis=0), shard, rep, False)
    w_mid = gather_weight(jnp.concatenate([ffn_gate, ffn_up], axis=1), shard, rep, False)
    w_down = gather_weight(ffn_down, shard, rep, False)
    mixer_rows_of = DS // 4
    ff = w_mid.shape[1] // 2

    token_rows = tokens.shape[0]
    batch_count = token_rows // SEQUENCE_LENGTH
    shard_groups = QUERY_HEADS // KEY_VALUE_HEADS
    inputs = tokens.astype(F32)
    norm_one, norm_one_back = jax.vjp(rms_scale, inputs, gain_one)
    normalized_input = norm_one.astype(BF)
    projected = matmul(normalized_input, w_in)
    gate_in = projected[:, GATE_AT:MIXED_AT]
    mixed_in = projected[:, MIXED_AT:Q_AT]
    step_in = projected[:, STEP_AT : STEP_AT + HM]

    def mixer_rows(
        gate_part,
        mixed_part,
        step_part,
        kernel_taps,
        kernel_offset,
        step_offset,
        decay_rates,
        skip_scale,
        norm_gain,
    ):
        value = mixer_core(
            gate_part.reshape(batch_count, SEQUENCE_LENGTH, -1),
            mixed_part.reshape(batch_count, SEQUENCE_LENGTH, -1),
            step_part.reshape(batch_count, SEQUENCE_LENGTH, -1),
            kernel_taps,
            kernel_offset,
            step_offset,
            decay_rates,
            skip_scale,
            norm_gain,
        )
        return value.reshape(token_rows, -1)

    mixer_value, mixer_back = jax.vjp(
        mixer_rows,
        gate_in,
        mixed_in,
        step_in,
        taps,
        offset,
        step_offset,
        decay_rates,
        skip_scale,
        gain_mixer,
    )
    mixer_norm = mixer_value.astype(BF)
    query_reduced = projected[:, Q_AT:K_AT].astype(BF)
    key_reduced = projected[:, K_AT:V_AT].astype(BF)
    value_reduced = projected[:, V_AT:STEP_AT].astype(BF)
    query_head_rows = query_reduced.reshape(
        batch_count, SEQUENCE_LENGTH, KEY_VALUE_HEADS, shard_groups, HEAD_WIDTH
    )
    key_head_rows = key_reduced.reshape(batch_count, SEQUENCE_LENGTH, KEY_VALUE_HEADS, HEAD_WIDTH)
    value_head_rows = value_reduced.reshape(
        batch_count, SEQUENCE_LENGTH, KEY_VALUE_HEADS, HEAD_WIDTH
    )
    scores = attention_scores(query_head_rows, key_head_rows, SEQUENCE_LENGTH)
    row_top = jnp.max(scores, axis=-1, keepdims=True)
    unscaled = jnp.exp(scores - row_top)
    row_total = jnp.sum(unscaled, axis=-1, keepdims=True)
    shares = unscaled / row_total
    shares_low = shares.astype(BF)
    context = jnp.einsum(
        "bkjqs,bskd->bqkjd", shares_low, value_head_rows, preferred_element_type=F32
    )
    context_low = context.reshape(token_rows, QW).astype(BF)
    out_side = jnp.concatenate(
        [mixer_norm.reshape(token_rows, 4, -1), context_low.reshape(token_rows, 4, -1)], axis=2
    ).reshape(token_rows, -1)
    middle = inputs + matmul(out_side, w_out)
    norm_two, norm_two_back = jax.vjp(rms_scale, middle, gain_two)
    normed_two = norm_two.astype(BF)
    mid = matmul(normed_two, w_mid)
    activated, swiglu_back = jax.vjp(swiglu, mid[:, :ff], mid[:, ff:])
    activated_low = activated.astype(BF)
    output = (middle + matmul(activated_low, w_down)).astype(BF)

    grad_activated = input_gradient(cotangent, w_down)
    grad_gate_wide, grad_up_wide = swiglu_back(grad_activated)
    grad_mid = jnp.concatenate([grad_gate_wide, grad_up_wide], axis=1).astype(BF)
    grad_normed_two = input_gradient(grad_mid, w_mid)
    grad_middle_norm, grad_gain_two = norm_two_back(grad_normed_two)
    grad_middle = cotangent.astype(F32) + grad_middle_norm
    branch_gradient = grad_middle.astype(BF)
    grad_out_side = input_gradient(branch_gradient, w_out).reshape(token_rows, 4, -1)
    grad_mixer_norm = grad_out_side[:, :, :mixer_rows_of].reshape(token_rows, DS)
    grad_context = (
        grad_out_side[:, :, mixer_rows_of:]
        .astype(BF)
        .reshape(batch_count, SEQUENCE_LENGTH, KEY_VALUE_HEADS, shard_groups, HEAD_WIDTH)
    )
    grad_shares = jnp.einsum(
        "bqkjd,bskd->bkjqs", grad_context, value_head_rows, preferred_element_type=F32
    )
    value_gradient_full = jnp.einsum(
        "bkjqs,bqkjd->bskd", shares_low, grad_context, preferred_element_type=F32
    )
    grad_scores = shares * (grad_shares - jnp.sum(shares * grad_shares, axis=-1, keepdims=True))
    grad_raw = (grad_scores * HEAD_WIDTH ** (-0.5)).astype(BF)
    grad_query_wide = jnp.einsum(
        "bkjqs,bskd->bqkjd", grad_raw, key_head_rows, preferred_element_type=F32
    )
    key_gradient_full = jnp.einsum(
        "bkjqs,bqkjd->bskd", grad_raw, query_head_rows, preferred_element_type=F32
    )
    (
        grad_gate_in,
        grad_mixed_in,
        grad_step_in,
        grad_taps,
        grad_offset,
        grad_step_offset,
        grad_decay,
        grad_skip,
        grad_gain_mixer,
    ) = mixer_back(grad_mixer_norm)
    grad_projected = jnp.concatenate(
        [
            grad_gate_in.astype(BF),
            grad_mixed_in.astype(BF),
            grad_query_wide.reshape(token_rows, QW).astype(BF),
            key_gradient_full.reshape(token_rows, KW).astype(BF),
            value_gradient_full.reshape(token_rows, KW).astype(BF),
            jnp.pad(grad_step_in.astype(BF), ((0, 0), (0, IN_COLS - STEP_AT - HM))),
        ],
        axis=1,
    )
    grad_normed = input_gradient(grad_projected, w_in)
    grad_inputs_norm, grad_gain_one = norm_one_back(grad_normed)
    tokens_grad = (grad_middle + grad_inputs_norm).astype(BF)

    down = reduce_rep(group_columns(activated_low, shard), group_rows(cotangent), rep)
    mid_grad = reduce_rep(group_columns(normed_two, shard), group_rows(grad_mid), rep)
    out_columns = group_columns(out_side, shard)
    group_tokens = out_columns.shape[0]
    out_columns = jnp.concatenate(
        [
            out_columns[:, :mixer_rows_of].reshape(group_tokens, reps, -1),
            out_columns[:, mixer_rows_of:].reshape(group_tokens, reps, -1),
        ],
        axis=2,
    ).reshape(group_tokens, -1)
    out_grad = reduce_rep(out_columns, group_rows(branch_gradient), rep)
    in_grad = reduce_rep(group_columns(normalized_input, shard), group_rows(grad_projected), rep)

    def blocks(vector):
        return vector.reshape(4, reps, -1)

    heads = jnp.concatenate(
        [grad_step_offset.reshape(4, -1), grad_decay.reshape(4, -1), grad_skip.reshape(4, -1)],
        axis=1,
    )
    small_grads = (
        blocks(grad_gain_one),
        grad_taps.reshape(KC, 4, reps, -1).transpose(1, 2, 0, 3).reshape(4, reps, -1),
        blocks(grad_offset),
        blocks(grad_gain_mixer),
        blocks(grad_gain_two),
        jnp.broadcast_to(heads[:, None, :], (4, reps, heads.shape[1])),
    )
    small_total = reduce_small(jnp.concatenate(small_grads, axis=2), shard, rep)
    smalls_out, at = [], 0
    for part in small_grads:
        smalls_out.append(small_total[at : at + part.shape[2]])
        at += part.shape[2]
    gain_one_out, taps_out, offset_out, gain_mixer_out, gain_two_out, heads_out = smalls_out
    each = HM // 4
    mixer_m = mixer_rows_of // reps
    return (
        output,
        tokens_grad,
        gain_one_out,
        in_grad[:, GATE_AT:MIXED_AT],
        in_grad[:, MIXED_AT:Q_AT],
        in_grad[:, STEP_AT : STEP_AT + HM],
        taps_out.reshape(KC, -1),
        offset_out,
        heads_out[:each],
        heads_out[each : 2 * each],
        heads_out[2 * each :],
        gain_mixer_out,
        out_grad[:mixer_m],
        in_grad[:, Q_AT:K_AT],
        in_grad[:, K_AT:V_AT],
        in_grad[:, V_AT:STEP_AT],
        out_grad[mixer_m:],
        gain_two_out,
        mid_grad[:, :ff],
        mid_grad[:, ff:],
        down,
    )


def solution(mesh):
    both = P(("shard", "rep"), None)
    rows, vector = P("shard", None), P("shard")
    owned = P(("shard", "rep"))
    return jax.shard_map(
        local,
        mesh=mesh,
        in_specs=(
            both,
            both,
            vector,
            rows,
            rows,
            rows,
            P(None, "shard"),
            vector,
            vector,
            vector,
            vector,
            vector,
            rows,
            rows,
            rows,
            rows,
            rows,
            vector,
            rows,
            rows,
            rows,
        ),
        out_specs=(
            both,
            both,
            owned,
            both,
            both,
            both,
            P(None, ("shard", "rep")),
            owned,
            vector,
            vector,
            vector,
            owned,
            both,
            both,
            both,
            both,
            both,
            owned,
            both,
            both,
            both,
        ),
        check_vma=False,
    )
```

time: 1460 us -> 1240 us (0.85)
  waiting for transfers between devices: 1160 us -> 167 us
  Pallas kernels: 0 us -> 778 us
  blocking collectives: 96.3 us -> 0 us
  local copies, waits for them, and re-layouts: 32.7 us -> 101 us
  starting transfers between devices: 1.84 us -> 66.8 us
  matrix products: 95.4 us -> 70.4 us
  between operations: 21.8 us -> 3.2 us
    reduce_scatter x21 -> x0, waiting for transfers between devices: 989 us -> none  [the longest x1 70.7 us: local(): lax.psum_scatter(owned[16], 'rep', scatter_dimension=0, tiled=True)]
    pallas_call x0 -> x4, Pallas kernels: none -> 778 us  [place(): pl.pallas_call(body, out_shape=jax.ShapeDtypeStruct((rows, columns), piec...]
    ppermute x0 -> x90, waiting for transfers between devices: none -> 167 us  [swap(): return lax.ppermute(value, axis, [(i, i ^ bit) for i in range(size)])]
    all_gather x8 -> x0, waiting for transfers between devices: 150 us -> none  [the longest x1 33.6 us: local(): lax.all_gather(ffn_up, 'shard', axis=0, tiled=True)]
    ppermute x0 -> x90, starting transfers between devices: none -> 66.8 us  [swap(): return lax.ppermute(value, axis, [(i, i ^ bit) for i in range(size)])]
    unnamed x3 -> x0, blocking collectives: 55.5 us -> none
    all_gather x7 -> x0, blocking collectives: 40.8 us -> none  [the longest x1 7.64 us: local(): lax.all_gather(key_matrix, 'shard', axis=0, tiled=True)]
    convert_element_type x28 -> x6, other arithmetic: 28.3 us -> 5.11 us  [the longest x1 1.68 us: local(): tokens_grad = (grad_middle + grad_inputs_norm).astype(BF)]
  transfers between devices with their start and end apart: 31 -> 90, of which waited for: 26 -> 40; matrix products, arithmetic and copies ran while one was open for 9% -> 7% of each run, Pallas kernels for 0% -> 42%
where the time goes in v1:
time: 1240 us; the launch traced here: 1220 us
  Pallas kernels  778 us (63%)
  waiting for transfers between devices  167 us (13%)
  local copies, waits for them, and re-layouts  101 us (8%)
  matrix products  70.4 us (6%)
  starting transfers between devices  66.8 us (5%)
  other arithmetic  37.1 us (3%)
    pallas_call x4, Pallas kernels, place(): pl.pallas_call(body, out_shape=jax.ShapeDtypeStruct((rows, columns), piec...  778 us
    ppermute x90, waiting for transfers between devices, swap(): return lax.ppermute(value, axis, [(i, i ^ bit) for i in range(size)])  167 us
    ppermute x90, starting transfers between devices, swap(): return lax.ppermute(value, axis, [(i, i ^ bit) for i in range(size)])  66.8 us
  transfers between devices with their start and end apart: 90, of which 40 were waited for; matrix products, arithmetic and copies ran while one was open for 7% of the time, Pallas kernels for 42%

profile of v1, /device:TPU:0, one launch (start us, length us, event | category | flops | bytes accessed | tf_op | source)
XLA Modules:
  0.0 1224.2 jit_solution(17544390576953876318)
XLA Ops:
  1.6 4.8 concatenate.108
  6.4 3.0 collective-permute-start.1
  47.8 4.6 collective-permute-done.37.refs_5_
  57.5 4.0 collective-permute-done.15.refs_5_
  65.0 4.3 collective-permute-done.7.refs_6_
  69.3 10.9 collective-permute-done.4.refs_3_
  88.9 3.0 collective-permute-done.43.refs_11_
  97.5 11.9 collective-permute-done.26.refs_5_
  110.7 9.5 collective-permute-done.6.refs_5_
  123.8 4.0 collective-permute-done.27.refs_6_
  154.5 128.9 %place.5 = bf16[2048,1024]{1,0:T(8,128)(2,1)} custom-call(s32[12]{0:T(128)} %stack.127.refs_0_, bf16[512,1024]{1,0:T(8,128)(2,1)} %copy-done.16, bf16[512,1024]{1,0:T(8,128)(2,1)} %copy-done.39, bf16[128,1024]{1,0:T(8,128)(2,1)} %collective-permute-done.13.refs_3_, bf16[128,1024]{1,0:T(8,128)(2,1)} %copy-done.50, bf16[128,1024]{1,0:T(8,128)(2,1)} %copy-done.49, ...), custom_call_target="tpu_custom_call" | custom-call | bytes 8388608 | tf_op jit(solution)/shard_map/place/pallas_call | solution.py:145
  283.4 128.9 %place.7 = bf16[2048,1024]{1,0:T(8,128)(2,1)} custom-call(s32[12]{0:T(128)} %stack.127.refs_0_, bf16[512,1024]{1,0:T(8,128)(2,1)} %refs_1_.1, bf16[512,1024]{1,0:T(8,128)(2,1)} %copy-done.40, bf16[128,1024]{1,0:T(8,128)(2,1)} %collective-permute-done.35.refs_3_, bf16[128,1024]{1,0:T(8,128)(2,1)} %copy-done.48, bf16[128,1024]{1,0:T(8,128)(2,1)} %copy-done.47, ...), custom_call_target="tpu_custom_call" | custom-call | bytes 8388608 | tf_op jit(solution)/shard_map/place/pallas_call | solution.py:145
  412.4 256.0 %place.6 = bf16[1024,4096]{1,0:T(8,128)(2,1)} custom-call(s32[12]{0:T(128)} %stack.130.refs_0_, bf16[256,4096]{1,0:T(8,128)(2,1)} %constant_dynamic-update-slice_fusion.7.refs_1_, bf16[256,4096]{1,0:T(8,128)(2,1)} %collective-permute-done.23.refs_2_, bf16[64,4096]{1,0:T(8,128)(2,1)} %copy-done.55, bf16[64,4096]{1,0:T(8,128)(2,1)} %collective-permute-done.25.refs_4_, ...), custom_call_target="tpu_custom_call" | custom-call | bytes 16777216 | tf_op jit(solution)/shard_map/place/pallas_call | solution.py:145
  668.4 264.0 %place.4 = bf16[1024,4224]{1,0:T(8,128)(2,1)} custom-call(s32[10]{0:T(128)} %stack.114.refs_0_, bf16[256,4224]{1,0:T(8,128)(2,1)} %copy-done.6, bf16[256,4224]{1,0:T(8,128)(2,1)} %collective-permute-done.3.refs_2_, bf16[64,4224]{1,0:T(8,128)(2,1)} %copy-done.52, bf16[64,4224]{1,0:T(8,128)(2,1)} %copy-done.54, bf16[64,4224]{1,0:T(8,128)(2,1)} %copy-done.53, ...), custom_call_target="tpu_custom_call" | custom-call | bytes 17301504 | tf_op jit(solution)/shard_map/place/pallas_call | solution.py:145
  932.5 4.8 fusion.106
  944.2 5.0 fusion.7
  960.5 4.8 fusion.108
  967.9 3.5 multiply_reduce_fusion.8
  991.6 5.8 fusion.22
  1013.0 3.7 fusion.6
  1030.3 3.8 multiply_reduce_fusion.3
  1037.4 7.4 fusion.44
  1082.2 3.5 collective-permute-done.71
  1095.4 6.3 collective-permute-done.87
  1104.9 7.1 collective-permute-done.75
  1118.2 15.2 %collective-permute-done.55 = bf16[128,4224]{1,0:T(8,128)(2,1)S(1)} collective-permute-done((bf16[128,4224]{1,0:T(8,128)(2,1)S(1)}, bf16[128,4224]{1,0:T(8,128)(2,1)S(1)}, u32[]{:S(2)}, u32[]{:S(2)}) %collective-permute-start.55) | collective-permute-done | bytes 1081376 | tf_op jit(solution)/shard_map/ppermute | solution.py:103
  1140.3 3.7 collective-permute-done.69
  1147.6 18.1 %collective-permute-done.77 = bf16[128,4096]{1,0:T(8,128)(2,1)S(1)} collective-permute-done((bf16[128,4096]{1,0:T(8,128)(2,1)S(1)}, bf16[128,4096]{1,0:T(8,128)(2,1)S(1)}, u32[]{:S(2)}, u32[]{:S(2)}) %collective-permute-start.77) | collective-permute-done | bytes 1048608 | tf_op jit(solution)/shard_map/ppermute | solution.py:103
  1165.7 6.3 convolution_add_fusion.1
  1173.7 13.9 %collective-permute-done.57 = bf16[128,4224]{1,0:T(8,128)(2,1)S(1)} collective-permute-done((bf16[128,4224]{1,0:T(8,128)(2,1)S(1)}, bf16[128,4224]{1,0:T(8,128)(2,1)S(1)}, u32[]{:S(2)}, u32[]{:S(2)}) %collective-permute-start.57) | collective-permute-done | bytes 1081376 | tf_op jit(solution)/shard_map/ppermute | solution.py:103
  1191.2 16.3 %collective-permute-done.58 = bf16[2,32,4224]{2,1,0:T(8,128)(2,1)S(1)} collective-permute-done((bf16[2,32,4224]{2,1,0:T(8,128)(2,1)S(1)}, bf16[2,32,4224]{2,1,0:T(8,128)(2,1)S(1)}, u32[]{:S(2)}, u32[]{:S(2)}) %collective-permute-start.58) | collective-permute-done | bytes 540704 | tf_op jit(solution)/shard_map/ppermute | solution.py:103
  1208.7 11.8 collective-permute-done.59
  (661 shorter events, 241.8 us)
Async XLA Ops:
  9.4 34.6 %collective-permute-start.84 = (bf16[128,1024]{1,0:T(8,128)(2,1)}, bf16[128,1024]{1,0:T(8,128)(2,1)}, u32[]{:S(2)}, u32[]{:S(2)}) collective-permute-start(bf16[128,1024]{1,0:T(8,128)(2,1)} %param.22), channel_id=1, source_target_pairs={{0,8},{8,0},{16,24},{24,16},{1,9},{9,1},{17,25},{25,17},{2,10},{10... | collective-permute-start | bytes 786440 | tf_op jit(solution)/shard_map/ppermute | solution.py:103
  9.9 35.8 %collective-permute-start.85 = (bf16[128,1024]{1,0:T(8,128)(2,1)}, bf16[128,1024]{1,0:T(8,128)(2,1)}, u32[]{:S(2)}, u32[]{:S(2)}) collective-permute-start(bf16[128,1024]{1,0:T(8,128)(2,1)} %param.22), channel_id=1, source_target_pairs={{0,16},{8,24},{16,0},{24,8},{1,17},{9,25},{17,1},{25,9},{2,18},{10... | collective-permute-start | bytes 786440 | tf_op jit(solution)/shard_map/ppermute | solution.py:103
  11.6 25.6 %collective-permute-start.35 = (bf16[128,1024]{1,0:T(8,128)(2,1)}, bf16[128,1024]{1,0:T(8,128)(2,1)}, u32[]{:S(2)}, u32[]{:S(2)}) collective-permute-start(bf16[128,1024]{1,0:T(8,128)(2,1)} %constant_dynamic-slice_fusion.25), channel_id=1, source_target_pairs={{0,16},{8,24},{16,0},{24,8},{1,17},{9,25},{17,1},{25,9},{2,18},{10... | collective-permute-start | bytes 786440 | tf_op jit(solution)/shard_map/ppermute | solution.py:103
  24.0 23.1 %collective-permute-start.13 = (bf16[128,1024]{1,0:T(8,128)(2,1)}, bf16[128,1024]{1,0:T(8,128)(2,1)}, u32[]{:S(2)}, u32[]{:S(2)}) collective-permute-start(bf16[128,1024]{1,0:T(8,128)(2,1)} %constant_dynamic-slice_fusion.27), channel_id=1, source_target_pairs={{0,16},{8,24},{16,0},{24,8},{1,17},{9,25},{17,1},{25,9},{2,18},{10... | collective-permute-start | bytes 786440 | tf_op jit(solution)/shard_map/ppermute | solution.py:103
  42.7 21.5 %collective-permute-start.24 = (bf16[64,4096]{1,0:T(8,128)(2,1)}, bf16[64,4096]{1,0:T(8,128)(2,1)S(1)}, u32[]{:S(2)}, u32[]{:S(2)}) collective-permute-start(bf16[64,4096]{1,0:T(8,128)(2,1)} %constant_dynamic-slice_fusion.26), channel_id=1, source_target_pairs={{0,16},{8,24},{16,0},{24,8},{1,17},{9,25},{17,1},{25,9},{2,18},{10... | collective-permute-start | bytes 1572872 | tf_op jit(solution)/shard_map/ppermute | solution.py:103
  53.7 26.5 %collective-permute-start.4 = (bf16[64,4224]{1,0:T(8,128)(2,1)S(1)}, bf16[64,4224]{1,0:T(8,128)(2,1)S(1)}, u32[]{:S(2)}, u32[]{:S(2)}) collective-permute-start(bf16[64,4224]{1,0:T(8,128)(2,1)S(1)} %get-tuple-element.159), channel_id=1, source_target_pairs={{0,16},{8,24},{16,0},{24,8},{1,17},{9,25},{17,1},{25,9},{2,18},{10... | collective-permute-start | bytes 1622024 | tf_op jit(solution)/shard_map/ppermute | solution.py:103
  61.6 34.6 %collective-permute-start.12 = (bf16[512,1024]{1,0:T(8,128)(2,1)S(1)}, bf16[512,1024]{1,0:T(8,128)(2,1)S(1)}, u32[]{:S(2)}, u32[]{:S(2)}) collective-permute-start(bf16[512,1024]{1,0:T(8,128)(2,1)S(1)} %constant_dynamic-update-slice_fusion.5.refs_1_), channel_id=1, source_target_pairs={{0,8},{8,0},{16,24},{24,16},{1,9},{9,1},{17,25},{25,17},{2,10},{10... | collective-permute-start | bytes 3145736 | tf_op jit(solution)/shard_map/ppermute | solution.py:103
  62.7 19.1 %collective-permute-start.38 = (bf16[64,1024]{1,0:T(8,128)(2,1)S(1)}, bf16[64,1024]{1,0:T(8,128)(2,1)S(1)}, u32[]{:S(2)}, u32[]{:S(2)}) collective-permute-start(bf16[64,1024]{1,0:T(8,128)(2,1)S(1)} %slice.298), channel_id=1, source_target_pairs={{0,1},{1,0},{2,3},{3,2},{4,5},{5,4},{6,7},{7,6},{8,9},{9,8},{10,11... | collective-permute-start | bytes 393224 | tf_op jit(solution)/shard_map/ppermute | solution.py:103
  64.2 19.2 %collective-permute-start.39 = (bf16[64,1024]{1,0:T(8,128)(2,1)S(1)}, bf16[64,1024]{1,0:T(8,128)(2,1)S(1)}, u32[]{:S(2)}, u32[]{:S(2)}) collective-permute-start(bf16[64,1024]{1,0:T(8,128)(2,1)S(1)} %slice.299), channel_id=1, source_target_pairs={{0,2},{1,3},{2,0},{3,1},{4,6},{5,7},{6,4},{7,5},{8,10},{9,11},{10,... | collective-permute-start | bytes 393224 | tf_op jit(solution)/shard_map/ppermute | solution.py:103
  69.3 17.6 %collective-permute-start.42 = (bf16[128,1024]{1,0:T(8,128)(2,1)S(1)}, bf16[128,1024]{1,0:T(8,128)(2,1)S(1)}, u32[]{:S(2)}, u32[]{:S(2)}) collective-permute-start(bf16[128,1024]{1,0:T(8,128)(2,1)S(1)} %collective-permute-done.37.refs_5_), channel_id=1, source_target_pairs={{0,8},{8,0},{16,24},{24,16},{1,9},{9,1},{17,25},{25,17},{2,10},{10... | collective-permute-start | bytes 786440 | tf_op jit(solution)/shard_map/ppermute | solution.py:103
  87.4 53.9 %collective-permute-start.23 = (bf16[256,4096]{1,0:T(8,128)(2,1)}, bf16[256,4096]{1,0:T(8,128)(2,1)}, u32[]{:S(2)}, u32[]{:S(2)}) collective-permute-start(bf16[256,4096]{1,0:T(8,128)(2,1)} %constant_dynamic-update-slice_fusion.7.refs_1_), channel_id=1, source_target_pairs={{0,8},{8,0},{16,24},{24,16},{1,9},{9,1},{17,25},{25,17},{2,10},{10... | collective-permute-start | bytes 6291464 | tf_op jit(solution)/shard_map/ppermute | solution.py:103
  96.2 572.2 %collective-permute-start.3 = (bf16[256,4224]{1,0:T(8,128)(2,1)S(1)}, bf16[256,4224]{1,0:T(8,128)(2,1)}, u32[]{:S(2)}, u32[]{:S(2)}) collective-permute-start(bf16[256,4224]{1,0:T(8,128)(2,1)S(1)} %pad_dynamic-update-slice_fusion.refs_1_), channel_id=1, source_target_pairs={{0,8},{8,0},{16,24},{24,16},{1,9},{9,1},{17,25},{25,17},{2,10},{10... | collective-permute-start | bytes 6488072 | tf_op jit(solution)/shard_map/ppermute | solution.py:103
  97.0 23.2 %collective-permute-start.6 = (bf16[64,4224]{1,0:T(8,128)(2,1)S(1)}, bf16[64,4224]{1,0:T(8,128)(2,1)S(1)}, u32[]{:S(2)}, u32[]{:S(2)}) collective-permute-start(bf16[64,4224]{1,0:T(8,128)(2,1)S(1)} %collective-permute-done.4.refs_3_), channel_id=1, source_target_pairs={{0,2},{1,3},{2,0},{3,1},{4,6},{5,7},{6,4},{7,5},{8,10},{9,11},{10,... | collective-permute-start | bytes 1622024 | tf_op jit(solution)/shard_map/ppermute | solution.py:103
  110.7 18.6 %collective-permute-start.31 = (bf16[64,4096]{1,0:T(8,128)(2,1)S(1)}, bf16[64,4096]{1,0:T(8,128)(2,1)S(1)}, u32[]{:S(2)}, u32[]{:S(2)}) collective-permute-start(bf16[64,4096]{1,0:T(8,128)(2,1)S(1)} %collective-permute-done.26.refs_5_), channel_id=1, source_target_pairs={{0,8},{8,0},{16,24},{24,16},{1,9},{9,1},{17,25},{25,17},{2,10},{10... | collective-permute-start | bytes 1572872 | tf_op jit(solution)/shard_map/ppermute | solution.py:103
  140.2 528.2 %collective-permute-start.8 = (bf16[64,4224]{1,0:T(8,128)(2,1)}, bf16[64,4224]{1,0:T(8,128)(2,1)}, u32[]{:S(2)}, u32[]{:S(2)}) collective-permute-start(bf16[64,4224]{1,0:T(8,128)(2,1)} %copy-done.52), channel_id=1, source_target_pairs={{0,8},{8,0},{16,24},{24,16},{1,9},{9,1},{17,25},{25,17},{2,10},{10... | collective-permute-start | bytes 1622024 | tf_op jit(solution)/shard_map/ppermute | solution.py:103
  140.8 527.6 %collective-permute-start.11 = (bf16[64,4224]{1,0:T(8,128)(2,1)}, bf16[64,4224]{1,0:T(8,128)(2,1)}, u32[]{:S(2)}, u32[]{:S(2)}) collective-permute-start(bf16[64,4224]{1,0:T(8,128)(2,1)} %copy-done.51), channel_id=1, source_target_pairs={{0,8},{8,0},{16,24},{24,16},{1,9},{9,1},{17,25},{25,17},{2,10},{10... | collective-permute-start | bytes 1622024 | tf_op jit(solution)/shard_map/ppermute | solution.py:103
  140.9 527.6 %collective-permute-start.10 = (bf16[64,4224]{1,0:T(8,128)(2,1)}, bf16[64,4224]{1,0:T(8,128)(2,1)}, u32[]{:S(2)}, u32[]{:S(2)}) collective-permute-start(bf16[64,4224]{1,0:T(8,128)(2,1)} %copy-done.53), channel_id=1, source_target_pairs={{0,8},{8,0},{16,24},{24,16},{1,9},{9,1},{17,25},{25,17},{2,10},{10... | collective-permute-start | bytes 1622024 | tf_op jit(solution)/shard_map/ppermute | solution.py:103
  141.3 527.1 %collective-permute-start.9 = (bf16[64,4224]{1,0:T(8,128)(2,1)}, bf16[64,4224]{1,0:T(8,128)(2,1)}, u32[]{:S(2)}, u32[]{:S(2)}) collective-permute-start(bf16[64,4224]{1,0:T(8,128)(2,1)} %copy-done.54), channel_id=1, source_target_pairs={{0,8},{8,0},{16,24},{24,16},{1,9},{9,1},{17,25},{25,17},{2,10},{10... | collective-permute-start | bytes 1622024 | tf_op jit(solution)/shard_map/ppermute | solution.py:103
  1052.0 20.3 %collective-permute-start.62 = (bf16[128,512]{1,0:T(8,128)(2,1)S(1)}, bf16[128,512]{1,0:T(8,128)(2,1)}, u32[]{:S(2)}, u32[]{:S(2)}) collective-permute-start(bf16[128,512]{1,0:T(8,128)(2,1)S(1)} %bitcast.394), channel_id=1, source_target_pairs={{0,16},{8,24},{16,0},{24,8},{1,17},{9,25},{17,1},{25,9},{2,18},{10... | collective-permute-start | bytes 393224 | tf_op jit(solution)/shard_map/ppermute | solution.py:103
  1052.9 23.2 %collective-permute-start.61 = (bf16[128,512]{1,0:T(8,128)(2,1)}, bf16[128,512]{1,0:T(8,128)(2,1)S(1)}, u32[]{:S(2)}, u32[]{:S(2)}) collective-permute-start(bf16[128,512]{1,0:T(8,128)(2,1)} %bitcast.117), channel_id=1, source_target_pairs={{0,16},{8,24},{16,0},{24,8},{1,17},{9,25},{17,1},{25,9},{2,18},{10... | collective-permute-start | bytes 393224 | tf_op jit(solution)/shard_map/ppermute | solution.py:103
  1054.0 22.3 %collective-permute-start.60 = (bf16[128,512]{1,0:T(8,128)(2,1)}, bf16[128,512]{1,0:T(8,128)(2,1)S(1)}, u32[]{:S(2)}, u32[]{:S(2)}) collective-permute-start(bf16[128,512]{1,0:T(8,128)(2,1)} %bitcast.393), channel_id=1, source_target_pairs={{0,8},{8,0},{16,24},{24,16},{1,9},{9,1},{17,25},{25,17},{2,10},{10... | collective-permute-start | bytes 393224 | tf_op jit(solution)/shard_map/ppermute | solution.py:103
  1085.7 26.4 %collective-permute-start.75 = (bf16[128,4096]{1,0:T(8,128)(2,1)}, bf16[128,4096]{1,0:T(8,128)(2,1)}, u32[]{:S(2)}, u32[]{:S(2)}) collective-permute-start(bf16[128,4096]{1,0:T(8,128)(2,1)} %pad_maximum_fusion.3), channel_id=1, source_target_pairs={{0,16},{8,24},{16,0},{24,8},{1,17},{9,25},{17,1},{25,9},{2,18},{10... | collective-permute-start | bytes 3145736 | tf_op jit(solution)/shard_map/ppermute | solution.py:103
  1090.7 46.6 %collective-permute-start.74 = (bf16[128,4096]{1,0:T(8,128)(2,1)}, bf16[128,4096]{1,0:T(8,128)(2,1)}, u32[]{:S(2)}, u32[]{:S(2)}) collective-permute-start(bf16[128,4096]{1,0:T(8,128)(2,1)} %pad_maximum_fusion.3), channel_id=1, source_target_pairs={{0,8},{8,0},{16,24},{24,16},{1,9},{9,1},{17,25},{25,17},{2,10},{10... | collective-permute-start | bytes 3145736 | tf_op jit(solution)/shard_map/ppermute | solution.py:103
  1091.3 42.2 %collective-permute-start.55 = (bf16[128,4224]{1,0:T(8,128)(2,1)S(1)}, bf16[128,4224]{1,0:T(8,128)(2,1)S(1)}, u32[]{:S(2)}, u32[]{:S(2)}) collective-permute-start(bf16[128,4224]{1,0:T(8,128)(2,1)S(1)} %copy-done.34), channel_id=1, source_target_pairs={{0,16},{8,24},{16,0},{24,8},{1,17},{9,25},{17,1},{25,9},{2,18},{10... | collective-permute-start | bytes 3244040 | tf_op jit(solution)/shard_map/ppermute | solution.py:103
  1094.0 18.3 %collective-permute-start.67 = (bf16[256,1024]{1,0:T(8,128)(2,1)S(1)}, bf16[256,1024]{1,0:T(8,128)(2,1)S(1)}, u32[]{:S(2)}, u32[]{:S(2)}) collective-permute-start(bf16[256,1024]{1,0:T(8,128)(2,1)S(1)} %convolution_convert_fusion.3), channel_id=1, source_target_pairs={{0,1},{1,0},{2,3},{3,2},{4,5},{5,4},{6,7},{7,6},{8,9},{9,8},{10,11... | collective-permute-start | bytes 1572872 | tf_op jit(solution)/shard_map/ppermute | solution.py:103
  1112.1 25.2 %collective-permute-start.76 = (bf16[128,4096]{1,0:T(8,128)(2,1)}, bf16[128,4096]{1,0:T(8,128)(2,1)S(1)}, u32[]{:S(2)}, u32[]{:S(2)}) collective-permute-start(bf16[128,4096]{1,0:T(8,128)(2,1)} %collective-permute-done.75), channel_id=1, source_target_pairs={{0,8},{8,0},{16,24},{24,16},{1,9},{9,1},{17,25},{25,17},{2,10},{10... | collective-permute-start | bytes 3145736 | tf_op jit(solution)/shard_map/ppermute | solution.py:103
  1114.0 19.4 %collective-permute-start.89 = (bf16[1,64,1024]{2,1,0:T(8,128)(2,1)S(1)}, bf16[1,64,1024]{2,1,0:T(8,128)(2,1)S(1)}, u32[]{:S(2)}, u32[]{:S(2)}) collective-permute-start(bf16[1,64,1024]{2,1,0:T(8,128)(2,1)S(1)} %dynamic-slice_convert_fusion.2), channel_id=1, source_target_pairs={{0,4},{1,5},{2,6},{3,7},{4,0},{5,1},{6,2},{7,3},{8,12},{9,13},{10,... | collective-permute-start | bytes 393224 | tf_op jit(solution)/shard_map/ppermute | solution.py:103
  1116.5 18.2 %collective-permute-start.68 = (bf16[2,64,1024]{2,1,0:T(8,128)(2,1)S(1)}, bf16[2,64,1024]{2,1,0:T(8,128)(2,1)S(1)}, u32[]{:S(2)}, u32[]{:S(2)}) collective-permute-start(bf16[2,64,1024]{2,1,0:T(8,128)(2,1)S(1)} %fusion.58), channel_id=1, source_target_pairs={{0,2},{1,3},{2,0},{3,1},{4,6},{5,7},{6,4},{7,5},{8,10},{9,11},{10,... | collective-permute-start | bytes 786440 | tf_op jit(solution)/shard_map/ppermute | solution.py:103
  1139.5 26.1 %collective-permute-start.77 = (bf16[128,4096]{1,0:T(8,128)(2,1)S(1)}, bf16[128,4096]{1,0:T(8,128)(2,1)S(1)}, u32[]{:S(2)}, u32[]{:S(2)}) collective-permute-start(bf16[128,4096]{1,0:T(8,128)(2,1)S(1)} %convolution_convert_fusion.1), channel_id=1, source_target_pairs={{0,1},{1,0},{2,3},{3,2},{4,5},{5,4},{6,7},{7,6},{8,9},{9,8},{10,11... | collective-permute-start | bytes 3145736 | tf_op jit(solution)/shard_map/ppermute | solution.py:103
  1146.8 40.8 %collective-permute-start.57 = (bf16[128,4224]{1,0:T(8,128)(2,1)S(1)}, bf16[128,4224]{1,0:T(8,128)(2,1)S(1)}, u32[]{:S(2)}, u32[]{:S(2)}) collective-permute-start(bf16[128,4224]{1,0:T(8,128)(2,1)S(1)} %convolution_convert_fusion), channel_id=1, source_target_pairs={{0,1},{1,0},{2,3},{3,2},{4,5},{5,4},{6,7},{7,6},{8,9},{9,8},{10,11... | collective-permute-start | bytes 3244040 | tf_op jit(solution)/shard_map/ppermute | solution.py:103
  1172.0 18.4 %collective-permute-start.78 = (bf16[2,32,4096]{2,1,0:T(8,128)(2,1)S(1)}, bf16[2,32,4096]{2,1,0:T(8,128)(2,1)S(1)}, u32[]{:S(2)}, u32[]{:S(2)}) collective-permute-start(bf16[2,32,4096]{2,1,0:T(8,128)(2,1)S(1)} %fusion.50), channel_id=1, source_target_pairs={{0,2},{1,3},{2,0},{3,1},{4,6},{5,7},{6,4},{7,5},{8,10},{9,11},{10,... | collective-permute-start | bytes 1572872 | tf_op jit(solution)/shard_map/ppermute | solution.py:103
  1188.8 18.7 %collective-permute-start.58 = (bf16[2,32,4224]{2,1,0:T(8,128)(2,1)S(1)}, bf16[2,32,4224]{2,1,0:T(8,128)(2,1)S(1)}, u32[]{:S(2)}, u32[]{:S(2)}) collective-permute-start(bf16[2,32,4224]{2,1,0:T(8,128)(2,1)S(1)} %fusion.42), channel_id=1, source_target_pairs={{0,2},{1,3},{2,0},{3,1},{4,6},{5,7},{6,4},{7,5},{8,10},{9,11},{10,... | collective-permute-start | bytes 1622024 | tf_op jit(solution)/shard_map/ppermute | solution.py:103
  (188 other events, 2707.5 us)
